TPU v7x, 256 devices: a whole 4x4x8 slice. The times are simulated.
256 devices in a mesh: grp: 2 (over x_lo), pt: 128 (over x_hi, y, z, core).
Axes of the slice: x: 4 (x_hi: 2, x_lo: 2; x = x_hi * 2 + x_lo), y: 4, z: 8, core: 2. Of those that a mesh axis runs over, the one named last changes fastest.
Arguments:
- left_factor: float32 [16, 128, 2048], P('grp', 'pt'), may hold values from 0 to 7340032, as said below
- right_factor: float32 [128, 128, 2048], P('grp', 'pt'), may hold values from 0 to 7340032, as said below
Outputs:
- product: float32 [16, 128, 4096], P('grp', 'pt')
Inputs may be any that keep to these rules, and one draw needn't show every extreme that they name: `left_factor`: every entry is a whole number, a residue modulo 7340033. `right_factor`: every entry is a whole number, a residue modulo 7340033.
All inputs are finite; a program needn't handle non-finite values.
Results may differ from a plain program's by a relative error of at most 0.0003.
Values sent between devices are 32-bit elements; how exact they have to be, the bound alone decides.
A program may use at most 64 MiB of HBM per device.

v0:
```python
import jax
import jax.numpy as jnp
import numpy as np
from jax import lax
from jax.sharding import PartitionSpec as P

FIRST = 32
SECOND = 128


modulus = 7340033


def root_powers(length_all):
    for generator in range(2, 64):
        candidate = pow(generator, (modulus - 1) // length_all, modulus)
        if pow(candidate, length_all // 2, modulus) == modulus - 1:
            break
    powers = [1]
    for counter in range(length_all - 1):
        powers.append(powers[-1] * candidate % modulus)
    return np.array(powers, dtype=np.int64)


def power_table(powers, exponents):
    return powers[exponents % powers.shape[0]]


def dft_tables():
    length_all = FIRST * SECOND
    powers = root_powers(length_all)
    half_first = np.arange(FIRST // 2)
    range_first = np.arange(FIRST)
    range_second = np.arange(SECOND)
    first_table = power_table(powers, SECOND * np.outer(half_first, range_first))
    twist_table = power_table(powers, np.outer(range_first, range_second))
    second_table = power_table(powers, FIRST * np.outer(range_second, range_second))
    back_first_table = power_table(powers, -FIRST * np.outer(range_second, range_second))
    back_twist_table = power_table(powers, -np.outer(range_second, range_first))
    scale_inv = pow(length_all, modulus - 2, modulus)
    back_second_table = (
        power_table(powers, -SECOND * np.outer(range_first, range_first)) * scale_inv % modulus
    )
    return (
        first_table,
        twist_table,
        second_table,
        back_first_table,
        back_twist_table,
        back_second_table,
    )


def stacked_table(table_np):
    pieces = [table_np // 256**limb_level % 256 for limb_level in range(3)]
    stacked = np.zeros((5, 3) + table_np.shape, dtype=np.float32)
    for total_level in range(5):
        for limb_level in range(3):
            partner = total_level - limb_level
            if 0 <= partner < 3:
                stacked[total_level, limb_level] = pieces[partner]
    return stacked


def limb_split(values):
    return [values % 256, values // 256 % 256, values // 65536]


def fold_sums(level_sums):
    result = level_sums[4] % modulus
    for limb_level in (3, 2, 1, 0):
        result = (result * 256 + level_sums[limb_level]) % modulus
    return result


def times_table(values, table_np):
    left_limbs = limb_split(values)
    right_limbs = limb_split(jnp.asarray(table_np.astype(np.int32)))
    level_sums = []
    for total_level in range(5):
        running = jnp.zeros_like(values)
        for limb_level in range(3):
            partner = total_level - limb_level
            if 0 <= partner < 3:
                running = running + left_limbs[limb_level] * right_limbs[partner]
        level_sums.append(running)
    return fold_sums(level_sums)


def limb_stack(values):
    return jnp.stack([piece.astype(jnp.bfloat16) for piece in limb_split(values)])


def contract(form, values, table_np):
    planes = jnp.einsum(
        form,
        limb_stack(values),
        jnp.asarray(stacked_table(table_np), jnp.bfloat16),
        preferred_element_type=jnp.float32,
    )
    return fold_sums([planes[limb_level].astype(jnp.int32) for limb_level in range(5)])


def forward(rows_in, tables):
    first_table, twist_table, second_table = (tables[0], tables[1], tables[2])
    entries = rows_in.shape[0]
    current = rows_in.reshape(entries, FIRST // 2, SECOND)
    current = contract("leab,slac->secb", current, first_table)
    current = times_table(current, twist_table)
    current = contract("lecb,slbd->sdce", current, second_table)
    return current.reshape(FIRST * SECOND, entries)


def inverse(point_values, tables):
    back_first_table, back_twist_table, back_second_table = (tables[3], tables[4], tables[5])
    entries = point_values.shape[1]
    current = point_values.reshape(SECOND, FIRST, entries)
    current = contract("ldce,sldb->sebc", current, back_first_table)
    current = times_table(current, back_twist_table)
    current = contract("lebc,slca->seab", current, back_second_table)
    return current.reshape(entries, FIRST * SECOND)


def multiply_points(left_points, right_points):
    planes = jnp.einsum(
        "xpik,ypjk->xypij",
        limb_stack(left_points),
        limb_stack(right_points),
        preferred_element_type=jnp.float32,
    )
    level_sums = []
    for total_level in range(5):
        running = jnp.zeros(planes.shape[2:], jnp.int32)
        for limb_level in range(3):
            partner = total_level - limb_level
            if 0 <= partner < 3:
                running = running + planes[limb_level, partner].astype(jnp.int32)
        level_sums.append(running)
    return fold_sums(level_sums)


def body(left_factor, right_factor):
    tables = dft_tables()
    length_all = FIRST * SECOND
    left_rows = left_factor.shape[0]
    inner_cols = left_factor.shape[1]
    right_rows = right_factor.shape[0]
    left_eval = forward(left_factor.astype(jnp.int32).reshape(-1, left_factor.shape[2]), tables)
    right_eval = forward(right_factor.astype(jnp.int32).reshape(-1, right_factor.shape[2]), tables)
    left_send = left_eval.astype(jnp.float32).reshape(length_all, left_rows, inner_cols)
    right_send = right_eval.astype(jnp.float32).reshape(length_all, right_rows, inner_cols)
    left_owned, right_owned = (
        lax.all_to_all(left_send, "pt", split_axis=0, concat_axis=2, tiled=True),
        lax.all_to_all(right_send, "pt", split_axis=0, concat_axis=2, tiled=True),
    )
    right_whole = lax.all_gather(right_owned, "grp", axis=1, tiled=True)
    product_points = multiply_points(left_owned.astype(jnp.int32), right_whole.astype(jnp.int32))
    returned = lax.all_to_all(
        product_points.astype(jnp.float32), "pt", split_axis=2, concat_axis=0, tiled=True
    )
    point_rows = returned.reshape(length_all, -1)
    coefficients = inverse(point_rows.astype(jnp.int32), tables)
    return (coefficients.astype(jnp.float32) / modulus).reshape(left_rows, inner_cols, length_all)


def solution(mesh):
    return jax.shard_map(
        body,
        mesh=mesh,
        in_specs=(P("grp", "pt", None), P("grp", "pt", None)),
        out_specs=P("grp", "pt", None),
        check_vma=False,
    )
```

profile of v0, /device:TPU:1, one launch (start us, length us, event | category | flops | bytes accessed | tf_op | source)
XLA Modules:
  0.0 229.2 jit_solution(4905200097810992016)
XLA Ops:
  9.9 9.1 %fusion.44 = (bf16[1,64,32,128]{3,2,0,1:T(8,128)(2,1)S(1)}, s32[1,64,32,128]{3,2,0,1:T(8,128)S(1)}) fusion(s32[32,128]{1,0:T(8,128)S(1)} %copy-done.8, s32[32,128]{1,0:T(8,128)S(1)} %copy-done.9, s32[32,128]{1,0:T(8,128)S(1)} %copy-done.10, f32[5,64,32,128]{3,2,0,1:T(8,128)S(1)} %convolution_bitcast_fusion), kind=kLoop, calls=%fused_computation.102 | loop fusion | flops 38273024 | bytes 6864896 | tf_op jit(solution)/shard_map/convert_element_type | solution.py:91
  19.0 1.6 fusion.46
  20.6 1.7 convolution_bitcast_fusion.1
  22.7 2.3 %slice_convert_fusion.3 = (s32[1,128,32,64]{1,2,0,3:T(8,128)}, s32[1,128,32,64]{1,2,0,3:T(8,128)}, s32[1,128,32,64]{1,2,0,3:T(8,128)}, s32[1,128,32,64]{1,2,0,3:T(8,128)}) fusion(f32[5,128,32,64]{1,2,0,3:T(8,128)S(1)} %convolution_bitcast_fusion.1), kind=kLoop, calls=%fused_computation.123 | loop fusion | flops 1048576 | bytes 8388608 | tf_op jit(solution)/shard_map/convert_element_type | solution.py:101
  25.0 3.0 %copy.141 = s32[1,128,32,64]{3,2,1,0:T(8,128)S(1)} copy(s32[1,128,32,64]{1,2,0,3:T(8,128)} %get-tuple-element.11) | data formatting | bytes 2097152 | tf_op jit(solution)/shard_map/convert_element_type | solution.py:101
  28.1 1.6 copy.142
  29.6 1.9 copy.136
  31.5 1.6 copy.137
  33.1 3.0 %copy.147 = s32[1,128,32,64]{3,2,1,0:T(8,128)S(1)} copy(s32[1,128,32,64]{1,2,0,3:T(8,128)} %get-tuple-element.12) | data formatting | bytes 2097152 | tf_op jit(solution)/shard_map/convert_element_type | solution.py:101
  36.1 1.6 copy.148
  37.7 1.9 copy.145
  39.6 1.6 copy.146
  41.1 2.1 copy.143
  43.2 1.6 copy.144
  44.8 5.2 %fusion.61 = f32[4096,64,1]{0,1,2:T(8,128)} fusion(s32[4096,64,1]{0,1,2:T(8,128)} %copy.148, s32[4096,64,1]{0,1,2:T(8,128)} %copy.146, s32[4096,64,1]{0,1,2:T(8,128)} %copy.144, s32[4096,64,1]{0,1,2:T(8,128)S(1)} %copy-done, s32[4096,64,1]{0,1,2:T(8,128)} %copy.137), kind=kLoop, calls=%fused_computation.119 | loop fusion | flops 9961472 | bytes 6291456 | tf_op jit(solution)/shard_map/convert_element_type | solution.py:151
  50.0 4.8 %copy.149 = f32[4096,64,1]{1,2,0:T(1,128)S(1)} copy(f32[4096,64,1]{0,1,2:T(8,128)} %fusion.61) | data formatting | bytes 2097152 | tf_op jit(solution)/shard_map/convert_element_type | solution.py:151
  55.4 19.4 %reduce = f32[4096,64]{1,0:T(8,128)} reduce(f32[4096,1,64]{2,1,0:T(1,128)S(1)} %bitcast.352, f32[]{:T(128)} %broadcast.2314), dimensions={1}, to_apply=%bitcast.334.reduce_sub_computation | reduce | bytes 2097156
  74.7 3.5 %reshape.1280 = f32[128,1,2048]{2,1,0:T(1,128)} reshape(f32[4096,64]{1,0:T(8,128)} %reduce) | data formatting | bytes 2097152
  78.2 16.4 %all-to-all-start = ((f32[128,1,2048]{2,1,0:T(1,128)}), f32[128,1,2048]{2,1,0:T(1,128)S(1)}, u32[]{:S(2)}, u32[]{:S(2)}) async-start(f32[128,1,2048]{2,1,0:T(1,128)} %reshape.1280), calls=%async_computation | async-start | bytes 2097152 | tf_op jit(solution)/shard_map/all_to_all | solution.py:154
  96.7 28.2 %all-to-all-done = f32[128,1,2048]{2,1,0:T(1,128)S(1)} async-done(((f32[128,1,2048]{2,1,0:T(1,128)}), f32[128,1,2048]{2,1,0:T(1,128)S(1)}, u32[]{:S(2)}, u32[]{:S(2)}) %all-to-all-start) | async-done | bytes 1048608 | tf_op jit(solution)/shard_map/all_to_all | solution.py:154
  124.9 3.1 %reduce.1 = f32[128,2048]{1,0:T(8,128)S(1)} reduce(f32[128,1,2048]{2,1,0:T(1,128)S(1)} %all-to-all-done, f32[]{:T(128)} %broadcast.2314), dimensions={1}, to_apply=%all_to_all.12.reduce_sub_computation | reduce | bytes 2097156 | tf_op jit(solution)/shard_map/all_to_all | solution.py:154
  128.1 2.6 %reshape.1281 = f32[4096,1,64]{2,1,0:T(1,128)S(1)} reshape(f32[128,2048]{1,0:T(8,128)S(1)} %reduce.1) | data formatting | bytes 2097152
  130.7 2.3 copy.150
  136.3 2.6 %copy.158 = f32[4096,8,1]{1,2,0:T(1,128)S(1)} copy(f32[4096,8,1]{0,1,2:T(8,128)S(1)} %fusion.141) | data formatting | bytes 262144 | tf_op jit(solution)/shard_map/convert_element_type | solution.py:150
  138.9 19.3 %reduce.2 = f32[4096,8]{1,0:T(8,128)} reduce(f32[4096,1,8]{2,1,0:T(1,128)S(1)} %bitcast.353, f32[]{:T(128)} %broadcast.2314), dimensions={1}, to_apply=%bitcast.336.reduce_sub_computation | reduce | bytes 262148
  158.3 2.8 %reshape.1282 = f32[128,1,256]{2,1,0:T(1,128)S(1)} reshape(f32[4096,8]{1,0:T(8,128)} %reduce.2) | data formatting | bytes 262144
  161.0 21.0 %all_to_all.36 = f32[128,1,256]{2,1,0:T(1,128)S(1)} all-to-all(f32[128,1,256]{2,1,0:T(1,128)S(1)} %reshape.1282), channel_id=1, replica_groups=mesh['grp'=2,'pt'=128] {'pt'}, dimensions={0} | all-to-all | bytes 262144 | tf_op jit(solution)/shard_map/all_to_all | solution.py:153
  183.0 3.5 %reshape.1283 = f32[4096,1,8]{2,1,0:T(1,128)S(1)} reshape(f32[128,256]{1,0:T(8,128)S(1)} %reduce.3) | data formatting | bytes 262144
  186.5 1.9 copy.159
  189.1 5.1 %fusion.68 = (bf16[1,32,128,128]{3,2,0,1:T(8,128)(2,1)S(1)}, bf16[1,32,128,128]{3,2,0,1:T(8,128)(2,1)S(1)}, bf16[1,32,128,128]{3,2,0,1:T(8,128)(2,1)S(1)}) fusion(f32[32,128,128,1]{2,1,0,3:T(8,128)} %all-gather.3.cloned.1.call-done), kind=kLoop, calls=%fused_computation.139 | loop fusion | flops 23068672 | bytes 5242880 | tf_op jit(solution)/shard_map/stack | solution.py:91
  196.5 18.5 %all_to_all.37 = f32[128,1,256]{2,1,0:T(1,128)S(1)} all-to-all(f32[128,1,256]{2,1,0:T(1,128)S(1)} %reshape.1284), channel_id=1, replica_groups=mesh['grp'=2,'pt'=128] {'pt'}, dimensions={0} | all-to-all | bytes 262144 | tf_op jit(solution)/shard_map/all_to_all | solution.py:158
  218.8 3.3 %fusion.205 = f32[8,1,4096]{2,1,0:T(1,128)} fusion(s32[8,1,4096]{2,1,0:T(1,128)S(1)} %bitcast.361, s32[8,1,4096]{2,1,0:T(1,128)S(1)} %bitcast.362, s32[8,1,4096]{2,1,0:T(1,128)S(1)} %bitcast.363, s32[8,1,4096]{2,1,0:T(1,128)S(1)} %bitcast.360, s32[8,1,4096]{2,1,0:T(1,128)S(1)} %bitcast.359), kind=kLoop, calls=%fused_computation.394 | loop fusion | flops 1277952 | bytes 786432 | tf_op jit(solution)/shard_map/div | solution.py:163
  (77 shorter events, 16.9 us)
Async XLA Ops:
  6.5 2.4 %copy-start.6 = (bf16[5,3,16,32,1]{3,2,1,0,4:T(8,128)(2,1)S(1)}, bf16[5,3,16,32,1]{3,2,1,0,4:T(8,128)(2,1)}, u32[]{:S(2)}) copy-start(bf16[5,3,16,32,1]{3,2,1,0,4:T(8,128)(2,1)} %constant.674) | copy-start | bytes 46084
  8.9 0.9 copy-start.8
  8.9 0.9 copy-start.9
  8.9 0.9 copy-start.10
  19.0 1.6 copy-start.3
  36.1 1.6 copy-start.2
  39.5 1.6 copy-start.1
  43.2 1.6 copy-start
  74.7 20.3 %copy-start.11 = (f32[8,1,2048]{2,1,0:T(1,128)S(1)}, f32[8,1,2048]{2,1,0:T(1,128)}, u32[]{:S(2)}) copy-start(f32[8,1,2048]{2,1,0:T(1,128)} %param.11) | copy-start | bytes 196612
  78.2 46.7 %all-to-all-start = ((f32[128,1,2048]{2,1,0:T(1,128)}), f32[128,1,2048]{2,1,0:T(1,128)S(1)}, u32[]{:S(2)}, u32[]{:S(2)}) async-start(f32[128,1,2048]{2,1,0:T(1,128)} %reshape.1280), calls=%async_computation | async-start | bytes 2097152 | tf_op jit(solution)/shard_map/all_to_all | solution.py:154
  94.6 94.5 %all-gather.3.cloned.1.call-start = ((), (), s32[]{:S(2)}) async-start(), calls=%async_computation.3 | async-start | bytes 3145728 | tf_op jit(solution)/shard_map/all_gather | solution.py:156
  130.7 2.5 %copy-start.4 = (bf16[5,3,128,128,1]{3,2,1,0,4:T(8,128)(2,1)S(1)}, bf16[5,3,128,128,1]{3,2,1,0,4:T(8,128)(2,1)}, u32[]{:S(2)}) copy-start(bf16[5,3,128,128,1]{3,2,1,0,4:T(8,128)(2,1)} %constant.675) | copy-start | bytes 1474564
  195.4 21.2 %copy-start.5 = (bf16[5,3,128,128,1]{3,2,1,0,4:T(8,128)(2,1)S(1)}, bf16[5,3,128,128,1]{3,2,1,0,4:T(8,128)(2,1)}, u32[]{:S(2)}) copy-start(bf16[5,3,128,128,1]{3,2,1,0,4:T(8,128)(2,1)} %constant.676) | copy-start | bytes 1474564
  196.2 20.8 %copy-start.12 = (s32[128,32]{0,1:T(8,128)S(1)}, s32[128,32]{0,1:T(8,128)}, u32[]{:S(2)}) copy-start(s32[128,32]{0,1:T(8,128)} %constant.673) | copy-start | bytes 49156
  196.2 20.8 %copy-start.13 = (s32[128,32]{0,1:T(8,128)S(1)}, s32[128,32]{0,1:T(8,128)}, u32[]{:S(2)}) copy-start(s32[128,32]{0,1:T(8,128)} %constant.669) | copy-start | bytes 49156
  196.2 20.8 %copy-start.14 = (s32[128,32]{0,1:T(8,128)S(1)}, s32[128,32]{0,1:T(8,128)}, u32[]{:S(2)}) copy-start(s32[128,32]{0,1:T(8,128)} %constant.648) | copy-start | bytes 49156
  216.1 2.3 copy-start.7
Sparse Core Ops, SparseCore 0:
  133.1 33.3 all-gather.2
where the time goes:
time: 233 us; the launch traced here: 229 us
  other arithmetic  77.6 us (33%)
  local copies, waits for them, and re-layouts  47.7 us (20%)
  blocking collectives  39.6 us (17%)
  waiting for transfers between devices  28.3 us (12%)
  starting transfers between devices  16.8 us (7%)
  between operations  14.3 us (6%)
  matrix products  5.01 us (2%)
    unnamed x2, other arithmetic  38.7 us
    all_to_all x1, waiting for transfers between devices, body(): lax.all_to_all(right_send, 'pt', split_axis=0, concat_axis=2, tiled=True)  28.2 us
    all_to_all x1, blocking collectives, body(): lax.all_to_all(left_send, 'pt', split_axis=0, concat_axis=2, tiled=True)  21 us
    all_to_all x1, blocking collectives, body(): lax.all_to_all(product_points.astype(jnp.float32), 'pt', split_axis=2, co...  18.5 us
    convert_element_type x16, local copies, waits for them, and re-layouts, contract(): planes[limb_level].astype(jnp.int32)  18 us
    all_to_all x1, starting transfers between devices, body(): lax.all_to_all(right_send, 'pt', split_axis=0, concat_axis=2, tiled=True)  16.4 us
    convert_element_type x10, other arithmetic, limb_stack(): piece.astype(jnp.bfloat16)  14.9 us
    unnamed x37, local copies, waits for them, and re-layouts  13.4 us
  transfers between devices with their start and end apart: 2, of which 1 were waited for; matrix products, arithmetic and copies ran while one was open for 16% of the time, Pallas kernels for 0%

commit v1 on v0

v1 whole, which is shorter than its diff:
```python
import functools

import jax
import jax.numpy as jnp
import ml_dtypes
import numpy as np
from jax import lax
from jax.experimental import pallas as pl
from jax.experimental.pallas import tpu as pltpu
from jax.sharding import PartitionSpec as P

FIRST = 32
SECOND = 128
LENGTH = FIRST * SECOND
HALF = FIRST // 2
MESH = pl.DeviceIdType.MESH

modulus = 7340033


def root_powers(length_all):
    for generator in range(2, 64):
        candidate = pow(generator, (modulus - 1) // length_all, modulus)
        if pow(candidate, length_all // 2, modulus) == modulus - 1:
            break
    powers = [1]
    for counter in range(length_all - 1):
        powers.append(powers[-1] * candidate % modulus)
    return np.array(powers, dtype=np.int64)


def table_digits(table_np):
    rows = []
    for level in range(3):
        value = table_np * pow(256, level, modulus) % modulus
        value = np.where(value > modulus // 2, value - modulus, value)
        low = (value + 128) % 256 - 128
        rest = (value - low) // 256
        mid = (rest + 128) % 256 - 128
        high = (rest - mid) // 256
        rows.append([piece * 2.0 ** (-8 * level) for piece in (low, mid, high)])
    return np.array(rows).swapaxes(0, 1)


@functools.cache
def tables():
    powers = root_powers(LENGTH)

    def power(exponents):
        return powers[exponents % LENGTH]

    def pack(array):
        return array.astype(np.float32).astype(ml_dtypes.bfloat16)

    a_half, a_all = np.arange(HALF), np.arange(FIRST)
    b_all = np.arange(SECOND)
    eye = np.eye(8)
    first = table_digits(power(SECOND * np.outer(a_all, a_half)))
    first = np.einsum("qlca,ef->qcelfa", first, eye)
    first = first.reshape(3, 8, 4, 8, 3 * 8 * HALF).swapaxes(0, 1).reshape(8, 96, 3 * 8 * HALF)
    expo = FIRST * np.outer(b_all, b_all)[None] + a_all[:, None, None] * b_all[None, None, :]
    second = table_digits(power(expo)).transpose(2, 0, 3, 1, 4).reshape(FIRST, 384, 384)
    third = table_digits(power(-expo)).transpose(2, 1, 3, 0, 4).reshape(FIRST, 384, 384)
    scale = pow(LENGTH, modulus - 2, modulus)
    fourth = table_digits(power(-SECOND * np.outer(a_all, a_all)) * scale % modulus)
    fourth = np.einsum("qlac,ij->qialcj", fourth, eye).reshape(768, 768)
    mask = (np.arange(SECOND)[None, None, :] % 8 == np.arange(8)[:, None, None]) * np.ones((8, 16, 1))
    return tuple(pack(item) for item in (first, second, third, fourth, mask))


def nearest(value):
    return (value + 12582912.0) - 12582912.0


def fold(low, mid, high):
    total = (high * 256.0 + mid) * 256.0 + low
    quotient = nearest(total * (1.0 / modulus))
    rest = mid + 256.0 * (high - 112.0 * quotient)
    return (low - quotient) + 256.0 * rest


def digits(value):
    high = (value + 1.5 * 2.0**39) - 1.5 * 2.0**39
    rest = value - high
    mid = (rest + 1.5 * 2.0**31) - 1.5 * 2.0**31
    return rest - mid, mid, high


def reduce_small(value):
    return value - float(modulus) * nearest(value * (1.0 / modulus))


def times_256(value):
    quotient = nearest(value * (256.0 / modulus))
    return (value * 256.0 - quotient * 7340032.0) - quotient


def narrow(value):
    return value.astype(jnp.bfloat16)


def dot(left, right, transposed=False):
    dims = (((1,), (1 if transposed else 0,)), ((), ()))
    return lax.dot_general(left, right, dims, preferred_element_type=jnp.float32)


def block_transpose(pieces):
    pieces = list(pieces)
    lane = lax.broadcasted_iota(jnp.int32, pieces[0].shape, 1)
    for bit in range(4):
        step, shift = 1 << bit, 8 << bit
        upper = (lane // shift) % 2 == 1
        for index in range(16):
            if index & step:
                continue
            one, two = pieces[index], pieces[index + step]
            pieces[index] = jnp.where(upper, pltpu.roll(two, shift, 1), one)
            pieces[index + step] = jnp.where(upper, two, pltpu.roll(one, SECOND - shift, 1))
    return pieces


CHAIN = ((4, 3), (3, 4))


def kernel(
    right_ref, left_ref, first_ref, second_hbm, third_hbm, fourth_hbm, mask_ref, out_ref,
    xdig, ysend, yrecv, second, third, fourth, ydig, rdig, ldig, pbuf, part, slots, usend, urecv,
    table_sem, send_sem, recv_sem, ring_send, ring_recv, back_send, back_recv,
):
    grp, pt = lax.axis_index("grp"), lax.axis_index("pt")
    core, z = lax.rem(pt, 2), lax.rem(pt // 2, 8)
    my_chunk = (pt // 64) * 4 + lax.rem(pt // 16, 4)
    me = my_chunk * 4 + core * 2 + grp

    def plane(chunk, inner):
        return (inner % 2, (chunk * 8 + z) * 2 + inner // 2)

    def ring(step):
        return (grp, (my_chunk * 8 + lax.rem(z + step + 8, 8)) * 2 + core)

    barrier = pltpu.get_barrier_semaphore()
    for offset in range(8):
        for inner in range(4):
            chunk = lax.rem(my_chunk + offset, 8)

            def greet():
                pl.semaphore_signal(barrier, inc=1, device_id=plane(chunk, inner), device_id_type=MESH)

            if offset == 0:
                pl.when(chunk * 4 + inner != me)(greet)
            else:
                greet()
    for step in (1, -1):
        pl.semaphore_signal(barrier, inc=1, device_id=ring(step), device_id_type=MESH)

    loads = [
        pltpu.make_async_copy(second_hbm.at[me], second, table_sem.at[0]),
        pltpu.make_async_copy(third_hbm.at[me], third, table_sem.at[1]),
        pltpu.make_async_copy(fourth_hbm, fourth, table_sem.at[2]),
    ]
    for load in loads:
        load.start()

    for group in range(9):
        if group < 8:
            block = jnp.concatenate([right_ref[pl.ds(y * 16 + group * 2, 2)] for y in range(4)], axis=0)
        else:
            block = left_ref[...]
        for level, piece in enumerate(digits(block.reshape(128, SECOND))):
            xdig[pl.ds(level * 128, 128), pl.ds(group * SECOND, SECOND)] = narrow(piece)

    pl.semaphore_wait(barrier, 33)

    def first_step(turn, carry):
        chunk = lax.rem(my_chunk + turn, 8)
        sums = dot(first_ref[chunk], xdig[...])
        folded = fold(sums[0:32], sums[32:64], sums[64:96])
        for inner in range(4):
            target = chunk * 4 + inner
            for group in range(9):
                ysend[target, pl.ds(group * 8, 8), :] = folded[
                    inner * 8 : inner * 8 + 8, group * SECOND : (group + 1) * SECOND
                ]

            @pl.when(target != me)
            def _():
                pltpu.make_async_remote_copy(
                    ysend.at[target], yrecv.at[me], send_sem, recv_sem.at[me],
                    device_id=plane(chunk, inner), device_id_type=MESH,
                ).start()

            @pl.when(target == me)
            def _():
                pltpu.make_async_copy(ysend.at[target], yrecv.at[me], recv_sem.at[me]).start()

        return carry

    lax.fori_loop(0, 8, first_step, 0)
    loads[0].wait()

    def second_step(turn, carry):
        chunk = lax.rem(my_chunk + 8 - turn, 8)
        for inner in range(4):
            source = chunk * 4 + inner
            pltpu.make_async_copy(yrecv.at[source], yrecv.at[source], recv_sem.at[source]).wait()
        values = yrecv[pl.ds(chunk * 4, 4), pl.ds(0, 64), :].reshape(256, SECOND)
        for level, piece in enumerate(digits(values)):
            ydig[:, pl.ds(level * SECOND, SECOND)] = narrow(piece)
        sums = dot(second[...], ydig[...], transposed=True)
        folded = fold(sums[0:128], sums[128:256], sums[256:384])
        for level, piece in enumerate(digits(folded)):
            piece = piece.reshape(16, 8, 256)
            both = jnp.concatenate([piece[:, :, :SECOND], piece[:, :, SECOND:]], axis=1)
            rdig[:, level, pl.ds(chunk * 16, 16), :] = narrow(both)
        return carry

    lax.fori_loop(0, 8, second_step, 0)

    values = yrecv[:, pl.ds(64, 8), :].reshape(256, SECOND)
    for level, piece in enumerate(digits(values)):
        ydig[:, pl.ds(level * SECOND, SECOND)] = narrow(piece)
    sums = dot(ydig[...], second[...], transposed=True)
    folded = fold(sums[:, 0:128], sums[:, 128:256], sums[:, 256:384])
    for group, piece in enumerate(block_transpose([folded[k * 16 : k * 16 + 16] for k in range(16)])):
        for level in range(3):
            low, mid, high = digits(piece)
            scale = 2.0 ** (-8 * level)
            ldig[group, 0, level] = narrow(low * scale)
            ldig[group, 1, level] = narrow(mid * (scale / 256.0))
            ldig[group, 2, level] = narrow(high * (scale / 65536.0))
            if level < 2:
                piece = times_256(piece)

    def multiply(group, carry):
        rows = []
        for digit in range(3):
            for d in range(8):
                rows.append(
                    jnp.concatenate([ldig[group, digit, level] * mask_ref[d] for level in range(3)], axis=1)
                )
        sums = dot(jnp.concatenate(rows, axis=0), rdig[group].reshape(384, SECOND))
        pbuf[pl.ds(group * 128, 128), :] = fold(sums[0:128], sums[128:256], sums[256:384])
        return carry

    lax.fori_loop(0, 16, multiply, 0)

    def turn_around(row, carry):
        part[row] = pbuf[pl.ds(row, 128, stride=16), :].T.reshape(2, 8, 8, SECOND)
        return carry

    lax.fori_loop(0, 16, turn_around, 0)

    def hop(half, way, step):
        length = CHAIN[half][way]
        sign = 1 if way == 0 else -1
        block = lax.rem(z + sign * (length - step + 1) + 8, 8)
        slot = (half * 2 + way) * 4 + step - 1
        return block, pltpu.make_async_remote_copy(
            part.at[pl.ds(half * 8, 8), :, block], slots.at[slot], ring_send.at[slot], ring_recv.at[slot],
            device_id=ring(sign), device_id_type=MESH,
        )

    sent = []
    for step in range(1, 5):
        for half in range(2):
            for way in range(2):
                if step > CHAIN[half][way]:
                    continue
                block, copy = hop(half, way, step)
                if step > 1:
                    slot = (half * 2 + way) * 4 + step - 2
                    sent[[item[0] for item in sent].index(slot)][1].wait_recv()
                    part[pl.ds(half * 8, 8), :, block] = part[pl.ds(half * 8, 8), :, block] + slots[slot]
                copy.start()
                sent.append(((half * 2 + way) * 4 + step - 1, copy))

    loads[1].wait()
    for half in range(2):
        total = part[pl.ds(half * 8, 8), :, z]
        for way in range(2):
            slot = (half * 2 + way) * 4 + CHAIN[half][way] - 1
            sent[[item[0] for item in sent].index(slot)][1].wait_recv()
            total = total + reduce_small(slots[slot])
        pieces = [narrow(piece) for piece in digits(total.reshape(128, SECOND))]
        sums = dot(jnp.concatenate(pieces, axis=1), third[...])
        usend[pl.ds(half * 8, 8)] = fold(sums[:, 0:128], sums[:, 128:256], sums[:, 256:384]).reshape(8, 16, SECOND)
        for offset in range(8):
            chunk = lax.rem(my_chunk + offset, 8)
            for core_to in range(2):
                inner = core_to * 2 + half
                row = (chunk // 4) * 8 + lax.rem(chunk, 4) * 2 + core_to
                source = usend.at[pl.ds(half * 8, 8), row]

                def give():
                    pltpu.make_async_remote_copy(
                        source, urecv.at[me], back_send, back_recv, device_id=plane(chunk, inner), device_id_type=MESH
                    ).start()

                def keep():
                    pltpu.make_async_copy(source, urecv.at[me], back_recv).start()

                if offset == 0:
                    pl.when(chunk * 4 + inner != me)(give)
                    pl.when(chunk * 4 + inner == me)(keep)
                else:
                    give()

    loads[2].wait()
    pltpu.make_async_copy(urecv, urecv, back_recv).wait()
    pieces = [narrow(piece) for piece in digits(urecv[...].reshape(256, SECOND))]
    sums = dot(fourth[...], jnp.concatenate(pieces, axis=0))
    folded = fold(sums[0:256], sums[256:512], sums[512:768])
    out_ref[...] = jnp.where(folded < 0, folded + float(modulus), folded)

    pltpu.make_async_copy(ysend.at[pl.ds(0, 31)], ysend.at[pl.ds(0, 31)], send_sem).wait()
    pltpu.make_async_copy(urecv.at[pl.ds(0, 31)], urecv.at[pl.ds(0, 31)], back_send).wait()
    for _, copy in sent:
        copy.wait_send()


def body(left_factor, right_factor):
    first, second, third, fourth, mask = (jnp.asarray(table) for table in tables())
    vmem = pl.BlockSpec(memory_space=pltpu.VMEM)
    hbm = pl.BlockSpec(memory_space=pltpu.HBM)
    f32, bf16 = jnp.float32, jnp.bfloat16
    dma = pltpu.SemaphoreType.DMA
    coefficients = pl.pallas_call(
        kernel,
        out_shape=jax.ShapeDtypeStruct((256, SECOND), f32),
        in_specs=[vmem, vmem, vmem, hbm, hbm, hbm, vmem],
        out_specs=vmem,
        scratch_shapes=[
            pltpu.VMEM((384, 9 * SECOND), bf16),
            pltpu.VMEM((32, 72, SECOND), f32),
            pltpu.VMEM((32, 72, SECOND), f32),
            pltpu.VMEM((384, 384), bf16),
            pltpu.VMEM((384, 384), bf16),
            pltpu.VMEM((768, 768), bf16),
            pltpu.VMEM((256, 384), bf16),
            pltpu.VMEM((16, 3, 128, SECOND), bf16),
            pltpu.VMEM((16, 3, 3, 16, SECOND), bf16),
            pltpu.VMEM((2048, SECOND), f32),
            pltpu.VMEM((16, 2, 8, 8, SECOND), f32),
            pltpu.VMEM((16, 8, 2, 8, SECOND), f32),
            pltpu.VMEM((16, 16, SECOND), f32),
            pltpu.VMEM((32, 8, SECOND), f32),
            dma((3,)),
            dma,
            dma((32,)),
            dma((16,)),
            dma((16,)),
            dma,
            dma,
        ],
        compiler_params=pltpu.CompilerParams(
            collective_id=0, has_side_effects=True, vmem_limit_bytes=48 * 1024 * 1024
        ),
    )(
        right_factor.reshape(64, HALF, SECOND), left_factor.reshape(8, HALF, SECOND),
        first, second, third, fourth, mask,
    )
    return coefficients.reshape(8, 1, LENGTH) / modulus


def solution(mesh):
    return jax.shard_map(
        body,
        mesh=mesh,
        in_specs=(P("grp", "pt", None), P("grp", "pt", None)),
        out_specs=P("grp", "pt", None),
        check_vma=False,
    )
```

time: 233 us -> 64.9 us (0.28); the launches traced: 229 us -> 64.6 us
  other arithmetic: 77.6 us -> 0.67 us
  Pallas kernels: 0 us -> 59 us
  local copies, waits for them, and re-layouts: 47.7 us -> 4.97 us
  blocking collectives: 39.6 us -> 0 us
  waiting for transfers between devices: 28.3 us -> 0 us
  starting transfers between devices: 16.8 us -> 0 us
  between operations: 14.3 us -> 0.01 us
  matrix products: 5.01 us -> 0 us
    pallas_call x0 -> x1, Pallas kernels: none -> 59 us  [body(): pl.pallas_call(kernel, out_shape=jax.ShapeDtypeStruct((256, SECOND), f32)...]
    all_to_all x2 -> x0, blocking collectives: 39.6 us -> none  [the longest x1 21 us: body(): lax.all_to_all(left_send, 'pt', split_axis=0, concat_axis=2, tiled=True)]
    unnamed x2 -> x0, other arithmetic: 38.7 us -> none
    all_to_all x1 -> x0, waiting for transfers between devices: 28.2 us -> none  [body(): lax.all_to_all(right_send, 'pt', split_axis=0, concat_axis=2, tiled=True)]
    convert_element_type x21 -> x0, local copies, waits for them, and re-layouts: 26.1 us -> none  [the longest x16 18 us: contract(): planes[limb_level].astype(jnp.int32)]
    convert_element_type x19 -> x0, other arithmetic: 24.8 us -> none  [the longest x10 14.9 us: limb_stack(): piece.astype(jnp.bfloat16)]
    all_to_all x1 -> x0, starting transfers between devices: 16.4 us -> none  [body(): lax.all_to_all(right_send, 'pt', split_axis=0, concat_axis=2, tiled=True)]
    unnamed x37 -> x10, local copies, waits for them, and re-layouts: 13.4 us -> 4.97 us
  transfers between devices with their start and end apart: 2 -> 0, of which waited for: 1 -> 0; matrix products, arithmetic and copies ran while one was open for 16% -> 0% of each run, Pallas kernels for 0% -> 0%
where the time goes in v1:
time: 64.9 us; the launch traced here: 64.6 us
  Pallas kernels  59 us (91%)
  local copies, waits for them, and re-layouts  4.97 us (8%)
  other arithmetic  0.67 us (1%)
    pallas_call x1, Pallas kernels, body(): pl.pallas_call(kernel, out_shape=jax.ShapeDtypeStruct((256, SECOND), f32)...  59 us
    unnamed x10, local copies, waits for them, and re-layouts  4.97 us

profile of v1, /device:TPU:1, one launch (start us, length us, event | category | flops | bytes accessed | tf_op | source)
XLA Modules:
  0.0 64.6 jit_solution(1505515822233017058)
XLA Ops:
  0.0 0.0 copy-start
  0.0 1.3 %copy-done = bf16[768,768]{1,0:T(8,128)(2,1)S(1)} copy-done((bf16[768,768]{1,0:T(8,128)(2,1)S(1)}, bf16[768,768]{1,0:T(8,128)(2,1)}, u32[]{:S(2)}) %copy-start) | copy-done | bytes 1179672
  1.3 0.0 copy-start.1
  1.3 1.1 %copy-done.1 = bf16[8,96,384]{2,1,0:T(8,128)(2,1)S(1)} copy-done((bf16[8,96,384]{2,1,0:T(8,128)(2,1)S(1)}, bf16[8,96,384]{2,1,0:T(8,128)(2,1)}, u32[]{:S(2)}) %copy-start.1) | copy-done | bytes 589848
  2.3 0.0 copy-start.2
  2.3 1.0 %copy-done.2 = f32[64,1,2048]{2,1,0:T(1,128)S(1)} copy-done((f32[64,1,2048]{2,1,0:T(1,128)S(1)}, f32[64,1,2048]{2,1,0:T(1,128)}, u32[]{:S(2)}) %copy-start.2) | copy-done | bytes 524312
  3.4 0.0 copy-start.3
  3.4 0.8 %copy-done.3 = f32[8,1,2048]{2,1,0:T(1,128)S(1)} copy-done((f32[8,1,2048]{2,1,0:T(1,128)S(1)}, f32[8,1,2048]{2,1,0:T(1,128)}, u32[]{:S(2)}) %copy-start.3) | copy-done | bytes 65560
  4.2 0.0 copy-start.4
  4.2 0.8 %copy-done.4 = bf16[8,16,128]{2,1,0:T(8,128)(2,1)S(1)} copy-done((bf16[8,16,128]{2,1,0:T(8,128)(2,1)S(1)}, bf16[8,16,128]{2,1,0:T(8,128)(2,1)}, u32[]{:S(2)}) %copy-start.4) | copy-done | bytes 32792
  5.0 59.0 %shard_map.73 = f32[256,128]{1,0:T(8,128)S(1)} custom-call(f32[64,16,128]{2,1,0:T(8,128)S(1)} %bitcast.3, f32[8,16,128]{2,1,0:T(8,128)S(1)} %bitcast.4, bf16[8,96,384]{2,1,0:T(8,128)(2,1)S(1)} %copy-done.1, bf16[32,384,384]{2,1,0:T(8,128)(2,1)} %constant.14.clone.second_hbm, bf16[32,384,384]{2,1,0:T(8,128)(2,1)} %constant.15.clone.third_hbm, ...), custom_call_target="tpu_custom_call" | custom-call | tf_op jit(solution)/shard_map/pallas_call | solution.py:327
  64.0 0.7 %broadcast_multiply_fusion = f32[256,128]{1,0:T(8,128)} fusion(f32[256,128]{1,0:T(8,128)S(1)} %shard_map.73), kind=kLoop, calls=%fused_computation | loop fusion | flops 32768 | bytes 262144 | tf_op jit(solution)/shard_map/div | solution.py:362
Async XLA Ops:
  0.0 1.3 %copy-start = (bf16[768,768]{1,0:T(8,128)(2,1)S(1)}, bf16[768,768]{1,0:T(8,128)(2,1)}, u32[]{:S(2)}) copy-start(bf16[768,768]{1,0:T(8,128)(2,1)} %constant.16.clone.fourth_hbm) | copy-start | bytes 3538948
  1.3 1.1 %copy-start.1 = (bf16[8,96,384]{2,1,0:T(8,128)(2,1)S(1)}, bf16[8,96,384]{2,1,0:T(8,128)(2,1)}, u32[]{:S(2)}) copy-start(bf16[8,96,384]{2,1,0:T(8,128)(2,1)} %constant.13.clone.first_ref) | copy-start | bytes 1769476
  2.3 1.0 %copy-start.2 = (f32[64,1,2048]{2,1,0:T(1,128)S(1)}, f32[64,1,2048]{2,1,0:T(1,128)}, u32[]{:S(2)}) copy-start(f32[64,1,2048]{2,1,0:T(1,128)} %param.8) | copy-start | bytes 1572868
  3.4 0.8 %copy-start.3 = (f32[8,1,2048]{2,1,0:T(1,128)S(1)}, f32[8,1,2048]{2,1,0:T(1,128)}, u32[]{:S(2)}) copy-start(f32[8,1,2048]{2,1,0:T(1,128)} %param.7) | copy-start | bytes 196612
  4.2 0.8 %copy-start.4 = (bf16[8,16,128]{2,1,0:T(8,128)(2,1)S(1)}, bf16[8,16,128]{2,1,0:T(8,128)(2,1)}, u32[]{:S(2)}) copy-start(bf16[8,16,128]{2,1,0:T(8,128)(2,1)} %constant.17.clone.mask_ref) | copy-start | bytes 98308

commit v2 on v1

v2 whole, which is shorter than its diff:
```python
import functools

import jax
import jax.numpy as jnp
import ml_dtypes
import numpy as np
from jax import lax
from jax.experimental import pallas as pl
from jax.experimental.pallas import tpu as pltpu
from jax.sharding import PartitionSpec as P

FIRST = 32
SECOND = 128
LENGTH = FIRST * SECOND
HALF = FIRST // 2
MESH = pl.DeviceIdType.MESH

modulus = 7340033


def root_powers(length_all):
    for generator in range(2, 64):
        candidate = pow(generator, (modulus - 1) // length_all, modulus)
        if pow(candidate, length_all // 2, modulus) == modulus - 1:
            break
    powers = [1]
    for counter in range(length_all - 1):
        powers.append(powers[-1] * candidate % modulus)
    return np.array(powers, dtype=np.int64)


def table_digits(table_np):
    rows = []
    for level in range(3):
        value = table_np * pow(256, level, modulus) % modulus
        value = np.where(value > modulus // 2, value - modulus, value)
        low = (value + 128) % 256 - 128
        rest = (value - low) // 256
        mid = (rest + 128) % 256 - 128
        high = (rest - mid) // 256
        rows.append([piece * 2.0 ** (-8 * level) for piece in (low, mid, high)])
    return np.array(rows).swapaxes(0, 1)


@functools.cache
def tables():
    powers = root_powers(LENGTH)

    def power(exponents):
        return powers[exponents % LENGTH]

    def pack(array):
        return array.astype(np.float32).astype(ml_dtypes.bfloat16)

    a_half, a_all = np.arange(HALF), np.arange(FIRST)
    b_all = np.arange(SECOND)
    eye = np.eye(8)
    first = table_digits(power(SECOND * np.outer(a_all, a_half)))
    first = np.einsum("qlca,ef->qcelfa", first, eye)
    first = first.reshape(3, 8, 4, 8, 3 * 8 * HALF).swapaxes(0, 1).reshape(8, 96, 3 * 8 * HALF)
    expo = FIRST * np.outer(b_all, b_all)[None] + a_all[:, None, None] * b_all[None, None, :]
    second = table_digits(power(expo)).transpose(2, 0, 3, 1, 4).reshape(FIRST, 384, 384)
    third = table_digits(power(-expo)).transpose(2, 1, 3, 0, 4).reshape(FIRST, 384, 384)
    scale = pow(LENGTH, modulus - 2, modulus)
    fourth = table_digits(power(-SECOND * np.outer(a_all, a_all)) * scale % modulus)
    fourth = np.einsum("qlac,ij->qialcj", fourth, eye).reshape(768, 768)
    return tuple(pack(item) for item in (first, second, third, fourth))


def nearest(value):
    return (value + 12582912.0) - 12582912.0


def fold(low, mid, high):
    total = (high * 256.0 + mid) * 256.0 + low
    quotient = nearest(total * (1.0 / modulus))
    rest = mid + 256.0 * (high - 112.0 * quotient)
    return (low - quotient) + 256.0 * rest


def digits(value):
    high = (value + 1.5 * 2.0**39) - 1.5 * 2.0**39
    rest = value - high
    mid = (rest + 1.5 * 2.0**31) - 1.5 * 2.0**31
    return rest - mid, mid, high


def reduce_small(value):
    return value - float(modulus) * nearest(value * (1.0 / modulus))


def times_256(value):
    quotient = nearest(value * (256.0 / modulus))
    return (value * 256.0 - quotient * 7340032.0) - quotient


def narrow(value):
    return value.astype(jnp.bfloat16)


def dot(left, right, transposed=False):
    dims = (((1,), (1 if transposed else 0,)), ((), ()))
    return lax.dot_general(left, right, dims, preferred_element_type=jnp.float32)


def block_transpose(pieces):
    pieces = list(pieces)
    lane = lax.broadcasted_iota(jnp.int32, pieces[0].shape, 1)
    for bit in range(4):
        step, shift = 1 << bit, 8 << bit
        upper = (lane // shift) % 2 == 1
        for index in range(16):
            if index & step:
                continue
            one, two = pieces[index], pieces[index + step]
            pieces[index] = jnp.where(upper, pltpu.roll(two, shift, 1), one)
            pieces[index + step] = jnp.where(upper, two, pltpu.roll(one, SECOND - shift, 1))
    return pieces


ORDER = [(dy, dc, dx) for dc in (0, 1) for dy in (2, 1, 3, 0) for dx in (2, 1, 3, 0)]
DELTA = (4, 3, -3, 2, -2, 1, -1, 0)
CHAIN = ((4, 3), (3, 4))


def kernel(
    right_hbm, left_hbm, first_hbm, second_hbm, third_hbm, fourth_hbm, out_ref,
    right_ref, left_ref, first_ref, xdig, send_one, send_two, recv_one, recv_two, second, third, fourth, ydig, rdig, ldig, pbuf, part, slots, usend, urecv,
    table_sem, send_sem, recv_sem, ring_send, ring_recv, back_send, back_recv,
):
    grp, pt = lax.axis_index("grp"), lax.axis_index("pt")
    core, z = lax.rem(pt, 2), lax.rem(pt // 2, 8)
    y, x = lax.rem(pt // 16, 4), (pt // 64) * 2 + grp
    my_chunk = y * 2 + core
    me = my_chunk * 4 + x

    def plane(chunk, inner):
        return (lax.rem(inner, 2), (((inner // 2) * 4 + chunk // 2) * 8 + z) * 2 + lax.rem(chunk, 2))

    def away(dy, dc):
        return lax.rem(y + dy, 4) * 2 + lax.rem(core + dc, 2)

    def ring(step):
        return (grp, (((x // 2) * 4 + y) * 8 + lax.rem(z + step + 8, 8)) * 2 + core)

    loads = [
        pltpu.make_async_copy(source, target, table_sem.at[index])
        for index, (source, target) in enumerate(
            (
                (right_hbm, right_ref), (left_hbm, left_ref), (first_hbm, first_ref),
                (second_hbm.at[me], second), (third_hbm.at[me], third), (fourth_hbm, fourth),
            )
        )
    ]
    for load in loads:
        load.start()

    barrier = pltpu.get_barrier_semaphore()
    for dy, dc, dx in ORDER:
        if (dy, dc, dx) != (0, 0, 0):
            pl.semaphore_signal(
                barrier, inc=1, device_id=plane(away(dy, dc), lax.rem(x + dx, 4)), device_id_type=MESH
            )
    for step in (1, -1):
        pl.semaphore_signal(barrier, inc=1, device_id=ring(step), device_id_type=MESH)

    for load in loads[:3]:
        load.wait()
    for group, delta in enumerate(DELTA[:4] + (None,) + DELTA[4:]):
        if delta is None:
            block = left_ref[...]
        else:
            plane_to = lax.rem(z + delta + 8, 8)
            block = jnp.concatenate([right_ref[pl.ds(row * 16 + plane_to * 2, 2)] for row in range(4)], axis=0)
        for level, piece in enumerate(digits(block.reshape(128, SECOND))):
            xdig[pl.ds(level * 128, 128), pl.ds(group * SECOND, SECOND)] = narrow(piece)

    pl.semaphore_wait(barrier, 33)

    shares = ((send_one, recv_one, 0, 5), (send_two, recv_two, 5, 4))
    for share, (sender, receiver, start, groups) in enumerate(shares):
        for dy, dc, _ in ORDER[::4]:
            chunk = away(dy, dc)
            sums = dot(first_ref[chunk], xdig[:, pl.ds(start * SECOND, groups * SECOND)])
            folded = fold(sums[0:32], sums[32:64], sums[64:96])
            for inner in range(4):
                for group in range(groups):
                    sender[chunk * 4 + inner, pl.ds(group * 8, 8), :] = folded[
                        inner * 8 : inner * 8 + 8, group * SECOND : (group + 1) * SECOND
                    ]
            for dx in (2, 1, 3, 0):
                inner = lax.rem(x + dx, 4)
                target = chunk * 4 + inner
                if (dy, dc, dx) != (0, 0, 0):
                    pltpu.make_async_remote_copy(
                        sender.at[target], receiver.at[me], send_sem.at[share], recv_sem.at[share, me],
                        device_id=plane(chunk, inner), device_id_type=MESH,
                    ).start()
                else:
                    pltpu.make_async_copy(sender.at[target], receiver.at[me], recv_sem.at[share, me]).start()

    loads[3].wait()

    def second_step(share):
        receiver = shares[share][1]
        for pair in range(4):
            chunks = [away(4 - dy, dc) for dy, dc, _ in ORDER[pair * 8 : pair * 8 + 8 : 4]]
            for place, chunk in enumerate(chunks):
                for inner in range(4):
                    source = chunk * 4 + inner
                    pltpu.make_async_copy(
                        receiver.at[source], receiver.at[source], recv_sem.at[share, source]
                    ).wait()
                values = receiver[pl.ds(chunk * 4, 4), pl.ds(0, 32), :].reshape(128, SECOND)
                for level, piece in enumerate(digits(values)):
                    ydig[pl.ds(place * 128, 128), pl.ds(level * SECOND, SECOND)] = narrow(piece)
            sums = dot(second[...], ydig[...], transposed=True)
            folded = fold(sums[0:128], sums[128:256], sums[256:384])
            for place, chunk in enumerate(chunks):
                near = folded[:, place * SECOND : (place + 1) * SECOND]
                both = jnp.concatenate(
                    [near.reshape(16, 8, SECOND), pltpu.roll(near, 64, 1).reshape(16, 8, SECOND)], axis=1
                )
                for level, piece in enumerate(digits(both)):
                    rdig[:, level, pl.ds(chunk * 16, 16), :] = narrow(piece)

    second_step(0)

    values = recv_one[:, pl.ds(32, 8), :].reshape(256, SECOND)
    for level, piece in enumerate(digits(values)):
        ydig[:, pl.ds(level * SECOND, SECOND)] = narrow(piece)
    sums = dot(ydig[...], second[...], transposed=True)
    folded = fold(sums[:, 0:128], sums[:, 128:256], sums[:, 256:384])
    for group, piece in enumerate(block_transpose([folded[k * 16 : k * 16 + 16] for k in range(16)])):
        for level in range(3):
            low, mid, high = digits(piece)
            scale = 2.0 ** (-8 * level)
            for digit, value in enumerate((low * scale, mid * (scale / 256.0), high * (scale / 65536.0))):
                for half in range(2):
                    rows = value[half * 8 : half * 8 + 8]
                    ldig[group, half, digit, level] = narrow(jnp.concatenate([rows, rows], axis=0))
            if level < 2:
                piece = times_256(piece)

    lane = lax.rem(lax.broadcasted_iota(jnp.int32, (16, SECOND), 1), 8)
    upper = lax.broadcasted_iota(jnp.int32, (16, SECOND), 0) // 8
    masks = [narrow(jnp.where(lane == 2 * pair + upper, 1.0, 0.0)) for pair in range(4)]

    def multiply(half):
        def one(group, carry):
            rows = []
            for digit in range(3):
                for d in range(0, 8, 2):
                    pair = [
                        jnp.concatenate([ldig[group, half, digit, level] * masks[d // 2] for level in range(3)], axis=1)
                    ]
                    rows += pair
            sums = dot(jnp.concatenate(rows, axis=0), rdig[group].reshape(384, SECOND))
            pbuf[half, pl.ds(group * 64, 64), :] = fold(sums[0:64], sums[64:128], sums[128:192])
            return carry

        lax.fori_loop(0, 16, one, 0, unroll=4)

    def turn_around(half, share):
        def one(row, carry):
            block = pbuf[half, pl.ds(row, 128, stride=8), :].T[:64].reshape(2, 4, 8, SECOND)
            part[half * 8 + row, :, pl.ds(share * 4, 4)] = block
            return carry

        lax.fori_loop(0, 8, one, 0, unroll=2)

    def hop(half, way, step):
        length = CHAIN[half][way]
        sign = 1 if way == 0 else -1
        delta = sign * (length - step + 1)
        block = DELTA.index(4 if delta == -4 else delta)
        slot = (half * 2 + way) * 4 + step - 1
        return block, pltpu.make_async_remote_copy(
            part.at[pl.ds(half * 8, 8), :, block], slots.at[slot], ring_send.at[slot], ring_recv.at[slot],
            device_id=ring(sign), device_id_type=MESH,
        )

    sent = {}

    def advance(half, step, ways=(0, 1)):
        for way in ways:
            if step > CHAIN[half][way]:
                continue
            block, copy = hop(half, way, step)
            if step > 1:
                sent[half, way, step - 1].wait_recv()
                slot = (half * 2 + way) * 4 + step - 2
                part[pl.ds(half * 8, 8), :, block] = part[pl.ds(half * 8, 8), :, block] + slots[slot]
            copy.start()
            sent[half, way, step] = copy

    multiply(0)
    turn_around(0, 0)
    advance(0, 1)
    multiply(1)
    turn_around(1, 0)
    advance(1, 1)
    second_step(1)
    advance(0, 2, (0,))
    multiply(0)
    turn_around(0, 1)
    advance(0, 2, (1,))
    advance(1, 2)
    multiply(1)
    turn_around(1, 1)
    advance(0, 3)
    advance(1, 3)
    advance(0, 4)
    advance(1, 4)

    loads[4].wait()
    for half in range(2):
        total = part[pl.ds(half * 8, 8), :, DELTA.index(0)]
        for way in range(2):
            slot = (half * 2 + way) * 4 + CHAIN[half][way] - 1
            sent[half, way, CHAIN[half][way]].wait_recv()
            total = total + reduce_small(slots[slot])
        pieces = [narrow(piece) for piece in digits(total.reshape(128, SECOND))]
        sums = dot(jnp.concatenate(pieces, axis=1), third[...])
        usend[pl.ds(half * 8, 8)] = fold(sums[:, 0:128], sums[:, 128:256], sums[:, 256:384]).reshape(8, 16, SECOND)
        for dy, dc, dx in ORDER:
            chunk, inner = away(dy, dc), (x // 2) * 2 + half
            if dx == 0:
                inner = lax.rem(inner, 4)
            elif dx == 2:
                inner = lax.rem(inner + 2, 4)
            else:
                continue
            source = usend.at[pl.ds(half * 8, 8), (inner // 2) * 8 + chunk]

            def give():
                pltpu.make_async_remote_copy(
                    source, urecv.at[me], back_send, back_recv, device_id=plane(chunk, inner), device_id_type=MESH
                ).start()

            def keep():
                pltpu.make_async_copy(source, urecv.at[me], back_recv).start()

            if (dy, dc, dx) == (0, 0, 0):
                pl.when(inner != x)(give)
                pl.when(inner == x)(keep)
            else:
                give()

    loads[5].wait()
    pltpu.make_async_copy(urecv, urecv, back_recv).wait()
    pieces = [narrow(piece) for piece in digits(urecv[...].reshape(256, SECOND))]
    sums = dot(fourth[...], jnp.concatenate(pieces, axis=0))
    folded = fold(sums[0:256], sums[256:512], sums[512:768])
    out_ref[...] = jnp.where(folded < 0, folded + float(modulus), folded)

    for share, (sender, _, _, _) in enumerate(shares):
        pltpu.make_async_copy(sender.at[pl.ds(0, 31)], sender.at[pl.ds(0, 31)], send_sem.at[share]).wait()
    pltpu.make_async_copy(urecv.at[pl.ds(0, 31)], urecv.at[pl.ds(0, 31)], back_send).wait()
    for copy in sent.values():
        copy.wait_send()


def body(left_factor, right_factor):
    first, second, third, fourth = (jnp.asarray(table) for table in tables())
    vmem = pl.BlockSpec(memory_space=pltpu.VMEM)
    hbm = pl.BlockSpec(memory_space=pltpu.HBM)
    f32, bf16 = jnp.float32, jnp.bfloat16
    dma = pltpu.SemaphoreType.DMA
    coefficients = pl.pallas_call(
        kernel,
        out_shape=jax.ShapeDtypeStruct((256, SECOND), f32),
        in_specs=[hbm] * 6,
        out_specs=vmem,
        scratch_shapes=[
            pltpu.VMEM((64, HALF, SECOND), f32),
            pltpu.VMEM((8, HALF, SECOND), f32),
            pltpu.VMEM((8, 96, 384), bf16),
            pltpu.VMEM((384, 9 * SECOND), bf16),
            pltpu.VMEM((32, 40, SECOND), f32),
            pltpu.VMEM((32, 32, SECOND), f32),
            pltpu.VMEM((32, 40, SECOND), f32),
            pltpu.VMEM((32, 32, SECOND), f32),
            pltpu.VMEM((384, 384), bf16),
            pltpu.VMEM((384, 384), bf16),
            pltpu.VMEM((768, 768), bf16),
            pltpu.VMEM((256, 384), bf16),
            pltpu.VMEM((16, 3, 128, SECOND), bf16),
            pltpu.VMEM((16, 2, 3, 3, 16, SECOND), bf16),
            pltpu.VMEM((2, 1024, SECOND), f32),
            pltpu.VMEM((16, 2, 8, 8, SECOND), f32),
            pltpu.VMEM((16, 8, 2, 8, SECOND), f32),
            pltpu.VMEM((16, 16, SECOND), f32),
            pltpu.VMEM((32, 8, SECOND), f32),
            dma((6,)),
            dma((2,)),
            dma((2, 32)),
            dma((16,)),
            dma((16,)),
            dma,
            dma,
        ],
        compiler_params=pltpu.CompilerParams(
            collective_id=0, has_side_effects=True, vmem_limit_bytes=48 * 1024 * 1024
        ),
    )(
        right_factor.reshape(64, HALF, SECOND), left_factor.reshape(8, HALF, SECOND),
        first, second, third, fourth,
    )
    return coefficients.reshape(8, 1, LENGTH) / modulus


def solution(mesh):
    return jax.shard_map(
        body,
        mesh=mesh,
        in_specs=(P("grp", "pt", None), P("grp", "pt", None)),
        out_specs=P("grp", "pt", None),
        check_vma=False,
    )
```

time: 64.9 us -> 51.4 us (0.79)
  Pallas kernels: 59 us -> 46.1 us
  local copies, waits for them, and re-layouts: 4.97 us -> 4.21 us
    pallas_call x1, Pallas kernels: 59 us -> 46.1 us  [body(): pl.pallas_call(kernel, out_shape=jax.ShapeDtypeStruct((256, SECOND), f32)...]
    unnamed x10 -> x8, local copies, waits for them, and re-layouts: 4.97 us -> 4.21 us
where the time goes in v2:
time: 51.4 us; the launch traced here: 51 us
  Pallas kernels  46.1 us (90%)
  local copies, waits for them, and re-layouts  4.21 us (8%)
  other arithmetic  0.67 us (1%)
    pallas_call x1, Pallas kernels, body(): pl.pallas_call(kernel, out_shape=jax.ShapeDtypeStruct((256, SECOND), f32)...  46.1 us
    unnamed x8, local copies, waits for them, and re-layouts  4.21 us

profile of v2, /device:TPU:1, one launch (start us, length us, event | category | flops | bytes accessed | tf_op | source)
XLA Modules:
  0.0 51.0 jit_solution(14444856822527679537)
XLA Ops:
  0.0 0.0 copy-start
  0.0 1.3 %copy-done = bf16[768,768]{1,0:T(8,128)(2,1)S(1)} copy-done((bf16[768,768]{1,0:T(8,128)(2,1)S(1)}, bf16[768,768]{1,0:T(8,128)(2,1)}, u32[]{:S(2)}) %copy-start) | copy-done | bytes 1179672
  1.3 0.0 copy-start.1
  1.3 1.1 %copy-done.1 = bf16[8,96,384]{2,1,0:T(8,128)(2,1)S(1)} copy-done((bf16[8,96,384]{2,1,0:T(8,128)(2,1)S(1)}, bf16[8,96,384]{2,1,0:T(8,128)(2,1)}, u32[]{:S(2)}) %copy-start.1) | copy-done | bytes 589848
  2.3 0.0 copy-start.2
  2.3 1.0 %copy-done.2 = f32[64,1,2048]{2,1,0:T(1,128)S(1)} copy-done((f32[64,1,2048]{2,1,0:T(1,128)S(1)}, f32[64,1,2048]{2,1,0:T(1,128)}, u32[]{:S(2)}) %copy-start.2) | copy-done | bytes 524312
  3.4 0.0 copy-start.3
  3.4 0.8 %copy-done.3 = f32[8,1,2048]{2,1,0:T(1,128)S(1)} copy-done((f32[8,1,2048]{2,1,0:T(1,128)S(1)}, f32[8,1,2048]{2,1,0:T(1,128)}, u32[]{:S(2)}) %copy-start.3) | copy-done | bytes 65560
  4.2 46.1 %shard_map.64 = f32[256,128]{1,0:T(8,128)S(1)} custom-call(f32[64,16,128]{2,1,0:T(8,128)S(1)} %bitcast.3, f32[8,16,128]{2,1,0:T(8,128)S(1)} %bitcast.4, bf16[8,96,384]{2,1,0:T(8,128)(2,1)S(1)} %copy-done.1, bf16[32,384,384]{2,1,0:T(8,128)(2,1)} %constant.12.clone.second_hbm, bf16[32,384,384]{2,1,0:T(8,128)(2,1)} %constant.13.clone.third_hbm, ...), custom_call_target="tpu_custom_call" | custom-call | tf_op jit(solution)/shard_map/pallas_call | solution.py:370
  50.4 0.7 %broadcast_multiply_fusion = f32[256,128]{1,0:T(8,128)} fusion(f32[256,128]{1,0:T(8,128)S(1)} %shard_map.64), kind=kLoop, calls=%fused_computation | loop fusion | flops 32768 | bytes 262144 | tf_op jit(solution)/shard_map/div | solution.py:410
Async XLA Ops:
  0.0 1.3 %copy-start = (bf16[768,768]{1,0:T(8,128)(2,1)S(1)}, bf16[768,768]{1,0:T(8,128)(2,1)}, u32[]{:S(2)}) copy-start(bf16[768,768]{1,0:T(8,128)(2,1)} %constant.14.clone.fourth_hbm) | copy-start | bytes 3538948
  1.3 1.1 %copy-start.1 = (bf16[8,96,384]{2,1,0:T(8,128)(2,1)S(1)}, bf16[8,96,384]{2,1,0:T(8,128)(2,1)}, u32[]{:S(2)}) copy-start(bf16[8,96,384]{2,1,0:T(8,128)(2,1)} %constant.11.clone.first_hbm) | copy-start | bytes 1769476
  2.3 1.0 %copy-start.2 = (f32[64,1,2048]{2,1,0:T(1,128)S(1)}, f32[64,1,2048]{2,1,0:T(1,128)}, u32[]{:S(2)}) copy-start(f32[64,1,2048]{2,1,0:T(1,128)} %param.7) | copy-start | bytes 1572868
  3.4 0.8 %copy-start.3 = (f32[8,1,2048]{2,1,0:T(1,128)S(1)}, f32[8,1,2048]{2,1,0:T(1,128)}, u32[]{:S(2)}) copy-start(f32[8,1,2048]{2,1,0:T(1,128)} %param.6) | copy-start | bytes 196612

commit v3 on v2

--- a/solution.py
+++ b/solution.py
@@ -120,6 +120,7 @@
 
 ORDER = [(dy, dc, dx) for dc in (0, 1) for dy in (2, 1, 3, 0) for dx in (2, 1, 3, 0)]
 DELTA = (4, 3, -3, 2, -2, 1, -1, 0)
+SHARES = ((0, 4), (4, 4))
 CHAIN = ((4, 3), (3, 4))
 
 
@@ -152,7 +153,7 @@
             )
         )
     ]
-    for load in loads:
+    for load in loads[:3]:
         load.start()
 
     barrier = pltpu.get_barrier_semaphore()
@@ -175,6 +176,7 @@
         for level, piece in enumerate(digits(block.reshape(128, SECOND))):
             xdig[pl.ds(level * 128, 128), pl.ds(group * SECOND, SECOND)] = narrow(piece)
 
+    ydig[...] = jnp.zeros_like(ydig)
     pl.semaphore_wait(barrier, 33)
 
     shares = ((send_one, recv_one, 0, 5), (send_two, recv_two, 5, 4))
@@ -198,11 +200,14 @@
                     ).start()
                 else:
                     pltpu.make_async_copy(sender.at[target], receiver.at[me], recv_sem.at[share, me]).start()
+        if share == 0:
+            for load in loads[3:]:
+                load.start()
 
     loads[3].wait()
 
     def second_step(share):
-        receiver = shares[share][1]
+        receiver, rows = shares[share][1], SHARES[share][1] * 8
         for pair in range(4):
             chunks = [away(4 - dy, dc) for dy, dc, _ in ORDER[pair * 8 : pair * 8 + 8 : 4]]
             for place, chunk in enumerate(chunks):
@@ -211,15 +216,15 @@
                     pltpu.make_async_copy(
                         receiver.at[source], receiver.at[source], recv_sem.at[share, source]
                     ).wait()
-                values = receiver[pl.ds(chunk * 4, 4), pl.ds(0, 32), :].reshape(128, SECOND)
+                values = receiver[pl.ds(chunk * 4, 4), pl.ds(0, rows), :].reshape(4 * rows, SECOND)
                 for level, piece in enumerate(digits(values)):
-                    ydig[pl.ds(place * 128, 128), pl.ds(level * SECOND, SECOND)] = narrow(piece)
+                    ydig[pl.ds(place * 128, 4 * rows), pl.ds(level * SECOND, SECOND)] = narrow(piece)
             sums = dot(second[...], ydig[...], transposed=True)
             folded = fold(sums[0:128], sums[128:256], sums[256:384])
             for place, chunk in enumerate(chunks):
                 near = folded[:, place * SECOND : (place + 1) * SECOND]
                 both = jnp.concatenate(
-                    [near.reshape(16, 8, SECOND), pltpu.roll(near, 64, 1).reshape(16, 8, SECOND)], axis=1
+                    [near.reshape(16, 8, SECOND), pltpu.roll(near, SECOND - 2 * rows, 1).reshape(16, 8, SECOND)], axis=1
                 )
                 for level, piece in enumerate(digits(both)):
                     rdig[:, level, pl.ds(chunk * 16, 16), :] = narrow(piece)
@@ -259,12 +264,14 @@
             pbuf[half, pl.ds(group * 64, 64), :] = fold(sums[0:64], sums[64:128], sums[128:192])
             return carry
 
-        lax.fori_loop(0, 16, one, 0, unroll=4)
+        lax.fori_loop(0, 16, one, 0, unroll=8)
 
     def turn_around(half, share):
+        start, count = SHARES[share]
+
         def one(row, carry):
-            block = pbuf[half, pl.ds(row, 128, stride=8), :].T[:64].reshape(2, 4, 8, SECOND)
-            part[half * 8 + row, :, pl.ds(share * 4, 4)] = block
+            turned = pbuf[half, pl.ds(row, 128, stride=8), :].T[: count * 16]
+            part[half * 8 + row, :, pl.ds(start, count)] = turned.reshape(2, count, 8, SECOND)
             return carry
 
         lax.fori_loop(0, 8, one, 0, unroll=2)
@@ -377,10 +384,7 @@
             pltpu.VMEM((8, HALF, SECOND), f32),
             pltpu.VMEM((8, 96, 384), bf16),
             pltpu.VMEM((384, 9 * SECOND), bf16),
-            pltpu.VMEM((32, 40, SECOND), f32),
-            pltpu.VMEM((32, 32, SECOND), f32),
-            pltpu.VMEM((32, 40, SECOND), f32),
-            pltpu.VMEM((32, 32, SECOND), f32),
+            *[pltpu.VMEM((32, rows, SECOND), f32) for rows in (40, 32, 40, 32)],
             pltpu.VMEM((384, 384), bf16),
             pltpu.VMEM((384, 384), bf16),
             pltpu.VMEM((768, 768), bf16),
@@ -401,7 +405,7 @@
             dma,
         ],
         compiler_params=pltpu.CompilerParams(
-            collective_id=0, has_side_effects=True, vmem_limit_bytes=48 * 1024 * 1024
+            collective_id=0, has_side_effects=True, vmem_limit_bytes=60 * 1024 * 1024
         ),
     )(
         right_factor.reshape(64, HALF, SECOND), left_factor.reshape(8, HALF, SECOND),

time: 51.4 us -> 47.2 us (0.918)
  local copies, waits for them, and re-layouts: 4.21 us -> 0 us
  other arithmetic: 0.67 us -> 1.57 us
    unnamed x8 -> x0, local copies, waits for them, and re-layouts: 4.21 us -> none
    div x1, other arithmetic: 0.67 us -> 1.57 us  [body(): return coefficients.reshape(8, 1, LENGTH) / modulus]
    pallas_call x1, Pallas kernels: 46.1 us -> 45.6 us  [body(): pl.pallas_call(kernel, out_shape=jax.ShapeDtypeStruct((256, SECOND), f32)...]
where the time goes in v3:
time: 47.2 us; the launch traced here: 47.1 us
  Pallas kernels  45.6 us (97%)
  other arithmetic  1.57 us (3%)
    pallas_call x1, Pallas kernels, body(): pl.pallas_call(kernel, out_shape=jax.ShapeDtypeStruct((256, SECOND), f32)...  45.6 us
    div x1, other arithmetic, body(): return coefficients.reshape(8, 1, LENGTH) / modulus  1.57 us

profile of v3, /device:TPU:1, one launch (start us, length us, event | category | flops | bytes accessed | tf_op | source)
XLA Modules:
  0.0 47.1 jit_solution(17096121540471810516)
XLA Ops:
  0.0 45.6 %shard_map.64 = f32[256,128]{1,0:T(8,128)} custom-call(f32[64,16,128]{2,1,0:T(8,128)} %bitcast.3, f32[8,16,128]{2,1,0:T(8,128)} %bitcast.4, bf16[8,96,384]{2,1,0:T(8,128)(2,1)} %constant.11.clone.first_hbm, bf16[32,384,384]{2,1,0:T(8,128)(2,1)} %constant.12.clone.second_hbm, bf16[32,384,384]{2,1,0:T(8,128)(2,1)} %constant.13.clone.third_hbm, ...), custom_call_target="tpu_custom_call" | custom-call | tf_op jit(solution)/shard_map/pallas_call | solution.py:377
  45.6 1.6 %broadcast_multiply_fusion = f32[256,128]{1,0:T(8,128)} fusion(f32[256,128]{1,0:T(8,128)} %shard_map.64), kind=kLoop, calls=%fused_computation | loop fusion | flops 32768 | bytes 262144 | tf_op jit(solution)/shard_map/div | solution.py:414
